TPU v7x, 256 devices: a whole 4x4x8 slice. The times are simulated.
256 devices in a mesh: dp: 32 (over y, z), expert: 8 (over x, core).
Axes of the slice: x: 4, y: 4, z: 8, core: 2. Of those that a mesh axis runs over, the one named last changes fastest.
Arguments:
- tokens: bfloat16 [2048, 3072], P('expert'), may hold values from -6 to 6
- cotangent: bfloat16 [2048, 3072], P('expert'), may hold values from -6 to 6
- routes: int32 [2048, 2], P('expert'), may hold values from 0 to 7, all different within a row; in each aligned block of 256 rows (0 to 255, 256 to 511, ...) at most 128 rows name the same one
- gate_values: bfloat16 [2048, 2], P('expert'), may hold values from 0.049804688 to 0.94921875
- gate_weight: bfloat16 [8, 3072, 8192], P('expert', None, 'dp'), may hold values from -0.109375 to 0.109375
- up_weight: bfloat16 [8, 3072, 8192], P('expert', None, 'dp'), may hold values from -0.109375 to 0.109375
- down_weight: bfloat16 [8, 3072, 8192], P('expert', None, 'dp'), may hold values from -0.0625 to 0.0625
Outputs:
- clipped: bfloat16 [8, 3, 3072, 8192], P('expert', None, 'dp')
- d_tokens: bfloat16 [3072, 2048], P('dp', 'expert')
Inputs may be any that keep to these rules, and one draw needn't show every extreme that they name: `routes`: each row names two different experts. Within the 256 rows of one device along expert (aligned blocks), no expert is named by more than 128 rows.
All inputs are finite; a program needn't handle non-finite values.
Results may differ from a plain program's by a relative error of at most 0.0064.
Values may be sent and summed in bfloat16 or wider, within the bound.
A program may use at most 128 MiB of HBM per device.

v0:
```python
import math
import jax
import jax.numpy as jnp
from jax import lax
from jax.sharding import PartitionSpec as P

CAP = 128
CLIP_RMS = 0.2


def slots_of(route_block, experts):
    flat_routes = route_block.reshape(-1)
    onehot = (flat_routes[:, None] == jnp.arange(experts, dtype=jnp.int32)[None, :]).astype(
        jnp.int32
    )
    before = jnp.cumsum(onehot, axis=0) - onehot
    position = jnp.sum(before * onehot, axis=1)
    counts = jnp.sum(onehot, axis=0)
    return (flat_routes * CAP + position, counts)


def fill_rows(token_block, cot_block, gate_block, slot_index, counts, experts):
    routed = slot_index.shape[0]
    row_of_slot = (
        jnp.zeros((experts * CAP,), jnp.int32)
        .at[slot_index]
        .set(jnp.arange(routed, dtype=jnp.int32))
    )
    live_slot = (jnp.arange(CAP, dtype=jnp.int32)[None, :] < counts[:, None]).reshape(-1)
    token_of_slot = row_of_slot // 2
    input_rows = jnp.where(
        live_slot[:, None], token_block[token_of_slot], jnp.zeros((), token_block.dtype)
    )
    scaled = gate_block.reshape(-1)[row_of_slot].astype(jnp.float32)[:, None] * cot_block[
        token_of_slot
    ].astype(jnp.float32)
    weighted_rows = jnp.where(live_slot[:, None], scaled, jnp.zeros((), scaled.dtype)).astype(
        jnp.bfloat16
    )
    model_width = token_block.shape[1]
    return (
        input_rows.reshape(experts, CAP, model_width),
        weighted_rows.reshape(experts, CAP, model_width),
    )


def row_contract(left, right):
    return lax.dot_general(
        left, right, (((0,), (0,)), ((), ())), preferred_element_type=jnp.float32
    )


def unit_contract(left, right):
    return lax.dot_general(
        left, right, (((1,), (1,)), ((), ())), preferred_element_type=jnp.float32
    )


def expert_pass(input_rows, weighted_rows, gate_matrix, up_matrix, down_matrix):
    pre_gate = jnp.dot(input_rows, gate_matrix, preferred_element_type=jnp.float32)
    pre_up = jnp.dot(input_rows, up_matrix, preferred_element_type=jnp.float32)
    sigmoid_gate = jax.nn.sigmoid(pre_gate)
    activated = pre_gate * sigmoid_gate
    hidden = (activated * pre_up).astype(jnp.bfloat16)
    grad_hidden = jnp.dot(weighted_rows, down_matrix, preferred_element_type=jnp.float32)
    grad_gate = (
        grad_hidden * pre_up * sigmoid_gate * (1.0 + pre_gate * (1.0 - sigmoid_gate))
    ).astype(jnp.bfloat16)
    grad_up = (grad_hidden * activated).astype(jnp.bfloat16)
    stacked = jnp.stack(
        [
            row_contract(input_rows, grad_gate),
            row_contract(input_rows, grad_up),
            row_contract(weighted_rows, hidden),
        ]
    )
    return (stacked, grad_gate, grad_up)


def per_device(tokens, cotangent, routes, gate_values, gate_weight, up_weight, down_weight):
    experts = lax.axis_size("expert")
    shards = lax.axis_size("dp")
    model_width = tokens.shape[1]
    gate_matrix = gate_weight[0]
    up_matrix = up_weight[0]
    down_matrix = down_weight[0]
    units = gate_matrix.shape[1]
    slot_index, counts = slots_of(routes, experts)
    input_send, weighted_send = fill_rows(
        tokens, cotangent, gate_values, slot_index, counts, experts
    )
    input_recv, weighted_recv, counts_recv = (
        lax.all_to_all(input_send, "expert", split_axis=0, concat_axis=0, tiled=True),
        lax.all_to_all(weighted_send, "expert", split_axis=0, concat_axis=0, tiled=True),
        lax.all_to_all(counts, "expert", split_axis=0, concat_axis=0, tiled=True),
    )
    slot_total = experts * CAP
    input_rows = input_recv.reshape(slot_total, model_width)
    weighted_rows = weighted_recv.reshape(slot_total, model_width)
    grad_sum, grad_gate, grad_up = expert_pass(
        input_rows, weighted_rows, gate_matrix, up_matrix, down_matrix
    )
    summed = lax.psum_scatter(
        unit_contract(gate_matrix, grad_gate) + unit_contract(up_matrix, grad_up),
        "dp",
        scatter_dimension=0,
        tiled=True,
    )
    returned_rows = lax.all_to_all(summed, "expert", split_axis=1, concat_axis=1, tiled=True)
    picked = returned_rows[:, slot_index]
    d_tokens = jnp.sum(picked.reshape(picked.shape[0], slot_index.shape[0] // 2, 2), axis=2).astype(
        jnp.bfloat16
    )
    gradients = grad_sum.astype(jnp.bfloat16)
    owned_rows = lax.all_to_all(gradients, "dp", split_axis=1, concat_axis=2, tiled=True)
    squares = lax.psum(jnp.sum(jnp.square(owned_rows.astype(jnp.float32))), ("dp", "expert"))
    clip_limit = CLIP_RMS * math.sqrt(3.0 * experts * model_width * units * shards)
    clip_scale = clip_limit / jnp.maximum(jnp.sqrt(squares), clip_limit)
    clipped = (owned_rows.astype(jnp.float32) * clip_scale).astype(jnp.bfloat16)
    return (clipped[None], d_tokens)


def solution(mesh):
    return jax.shard_map(
        per_device,
        mesh=mesh,
        in_specs=(
            P("expert", None),
            P("expert", None),
            P("expert", None),
            P("expert", None),
            P("expert", None, "dp"),
            P("expert", None, "dp"),
            P("expert", None, "dp"),
        ),
        out_specs=(P("expert", None, "dp", None), P("dp", "expert")),
        check_vma=False,
    )
```

profile of v0, /device:TPU:1, one launch (start us, length us, event | category | flops | bytes accessed | tf_op | source)
XLA Modules:
  0.0 574.3 jit_solution(8340505373630688563)
XLA Ops:
  7.2 0.0 copy-start
  7.2 0.8 broadcast_multiply_fusion
  8.0 0.8 copy.15
  8.8 0.1 eq.25
  8.9 0.1 eq.29
  9.1 0.1 copy.16
  9.2 0.1 mul.69
  9.4 1.1 reduce-window.6
  10.5 0.2 slice_reduce_fusion
  10.8 0.1 convert_reduce_fusion
  11.0 2.4 scatter_custom_fusion
  13.4 0.1 iota_compare_fusion.2
  13.5 13.8 %gather_fusion = bf16[1024,3072]{1,0:T(8,128)(2,1)} fusion(bf16[256,3072]{1,0:T(8,128)(2,1)} %param.7, s32[1024]{0:T(1024)S(1)} %get-tuple-element.9), kind=kCustom, calls=%fused_computation | custom fusion | bytes 12587008 | tf_op jit(solution)/shard_map/gather | solution.py:32
  27.3 5.9 %broadcast_select_fusion = bf16[8,128,3072]{2,1,0:T(8,128)(2,1)} fusion(bf16[8,128,3072]{2,1,0:T(8,128)(2,1)} %bitcast.59, pred[8,128]{1,0:T(8,128)(4,1)S(1)} %iota_compare_fusion.2), kind=kLoop, calls=%fused_computation.13 | loop fusion | flops 3145728 | bytes 12583936 | tf_op jit(solution)/shard_map/jit(_where)/select_n | solution.py:31
  33.2 8.0 %all-to-all-start = ((bf16[8,128,3072]{2,1,0:T(8,128)(2,1)}), bf16[8,128,3072]{2,1,0:T(8,128)(2,1)}, u32[]{:S(2)}, u32[]{:S(2)}) async-start(bf16[8,128,3072]{2,1,0:T(8,128)(2,1)} %broadcast_select_fusion), calls=%async_computation | async-start | bytes 12582912 | tf_op jit(solution)/shard_map/all_to_all | solution.py:93
  41.3 0.0 copy-done.2
  41.3 6.8 %gather_fusion.2 = bf16[1024,3072]{1,0:T(8,128)(2,1)} fusion(bf16[256,3072]{1,0:T(8,128)(2,1)S(1)} %copy-done.2, s32[1024]{0:T(1024)S(1)} %get-tuple-element.9), kind=kCustom, calls=%fused_computation.2 | custom fusion | bytes 12587008 | tf_op jit(solution)/shard_map/gather | solution.py:34
  48.1 0.0 copy-done.6
  48.1 0.1 copy.18
  48.3 0.2 reshape.131
  48.4 6.8 %gather_fusion.1 = bf16[1024]{0:T(1024)(128)(2,1)S(1)} fusion(bf16[512]{0:T(512)(128)(2,1)S(1)} %reshape.131, s32[1024]{0:T(1024)S(1)} %get-tuple-element.8), kind=kCustom, calls=%fused_computation.1 | custom fusion | bytes 8192 | tf_op jit(solution)/shard_map/gather | solution.py:34
  55.2 8.9 %fusion.3 = bf16[8,128,3072]{2,1,0:T(8,128)(2,1)} fusion(bf16[8,128,3072]{2,1,0:T(8,128)(2,1)} %bitcast.58, f32[8,128]{1,0:T(8,128)S(1)} %bitcast_convert_fusion, pred[8,128]{1,0:T(8,128)(4,1)S(1)} %iota_compare_fusion.2), kind=kLoop, calls=%fused_computation.11 | loop fusion | flops 12582912 | bytes 12588032 | tf_op jit(solution)/shard_map/convert_element_type | solution.py:37
  64.2 48.5 %all-to-all-done = bf16[8,128,3072]{2,1,0:T(8,128)(2,1)} async-done(((bf16[8,128,3072]{2,1,0:T(8,128)(2,1)}), bf16[8,128,3072]{2,1,0:T(8,128)(2,1)}, u32[]{:S(2)}, u32[]{:S(2)}) %all-to-all-start) | async-done | bytes 6291488 | tf_op jit(solution)/shard_map/all_to_all | solution.py:93
  112.7 5.5 all-to-all-start.1
  118.2 0.0 reduce-scatter.4.cloned.1.call-start
  118.2 0.0 copy-done.4
  118.2 5.5 fusion.12
  123.7 65.8 %all-to-all-done.1 = bf16[8,128,3072]{2,1,0:T(8,128)(2,1)} async-done(((bf16[8,128,3072]{2,1,0:T(8,128)(2,1)}), bf16[8,128,3072]{2,1,0:T(8,128)(2,1)}, u32[]{:S(2)}, u32[]{:S(2)}) %all-to-all-start.1) | async-done | bytes 6291488 | tf_op jit(solution)/shard_map/all_to_all | solution.py:94
  189.6 5.1 fusion.14
  194.7 0.0 copy-done
  194.7 0.0 copy-done.7
  194.7 5.8 %multiply_convert_fusion.2 = (bf16[1024,256]{1,0:T(8,128)(2,1)S(1)}, bf16[1024,256]{1,0:T(8,128)(2,1)S(1)}, f32[1024,256]{1,0:T(8,128)}) fusion(f32[1024,256]{1,0:T(8,128)S(1)} %fusion.14, f32[1024,256]{1,0:T(8,128)S(1)} %copy-done.7, bf16[1024,3072]{1,0:T(8,128)(2,1)} %bitcast.5, bf16[1,3072,256]{2,1,0:T(8,128)(2,1)S(1)} %copy-done), kind=kOutput, calls=%fused_computation.32 | convolution fusion | flops 1614020608 | bytes 12058624 | tf_op jit(solution)/shard_map/dot_general | solution.py:60
  200.5 1.8 fusion.7
  202.3 0.0 copy-done.5
  202.3 6.3 %add_bitcast_fusion = f32[3072,1024]{0,1:T(8,128)} fusion(f32[1024,3072]{1,0:T(8,128)S(1)} %fusion.7, bf16[1024,256]{1,0:T(8,128)(2,1)S(1)} %get-tuple-element.7, bf16[1,3072,256]{2,1,0:T(8,128)(2,1)S(1)} %copy-done.5), kind=kOutput, calls=%fused_computation.12 | convolution fusion | flops 1613758464 | bytes 27262976 | tf_op jit(solution)/shard_map/dot_general | solution.py:54
  208.6 12.6 %copy.24 = f32[3072,1024]{1,0:T(8,128)} copy(f32[3072,1024]{0,1:T(8,128)} %add_bitcast_fusion) | data formatting | bytes 25165824
  221.2 0.0 reduce-scatter.4.cloned.1.call-update
  221.2 4.7 fusion.5
  225.9 0.0 copy-start.8
  225.9 0.0 copy-start.9
  225.9 4.8 fusion.4
  230.8 0.0 copy-done.8
  230.8 0.0 copy-done.9
  230.8 5.2 fusion.6
  235.9 0.6 pad_maximum_fusion
  236.5 23.9 %copy.19 = bf16[3,3072,256]{2,0,1:T(4,128)(2,1)S(1)} copy(bf16[3,3072,256]{2,1,0:T(8,128)(2,1)S(1)} %pad_maximum_fusion) | data formatting | bytes 9437184 | tf_op jit(solution)/shard_map/stack | solution.py:70
  260.4 187.1 %all_to_all.31 = bf16[3,3072,256]{2,0,1:T(4,128)(2,1)S(1)} all-to-all(bf16[3,3072,256]{2,0,1:T(4,128)(2,1)S(1)} %copy.19), channel_id=1, replica_groups=mesh['dp'=32,'expert'=8] {'dp'}, dimensions={1} | all-to-all | bytes 9437184 | tf_op jit(solution)/shard_map/all_to_all | solution.py:115
  447.6 2.6 copy-done.3
  450.2 7.1 %fusion = f32[]{:T(128)} fusion(bf16[3,3072,256]{2,0,1:T(4,128)(2,1)S(1)} %all_to_all.31), kind=kLoop, calls=%fused_computation.7 | loop fusion | flops 7077887 | bytes 4718596 | tf_op jit(solution)/shard_map/reduce_sum | solution.py:116
  457.3 74.5 %psum.7 = f32[]{:T(128)} all-reduce(f32[]{:T(128)} %fusion), channel_id=1, replica_groups=mesh['dp'=32,'expert'=8] {'dp','expert'}, use_global_device_ids=true, to_apply=%region_6.7 | all-reduce | flops 1 | bytes 8 | tf_op jit(solution)/shard_map/psum | solution.py:116
  532.5 1.9 reduce-scatter.4.cloned.1.call-done
  534.5 1.2 copy.25
  535.6 1.0 copy.21
  536.6 9.1 %all-to-all-start.3 = ((f32[96,8,128]{2,0,1:T(8,128)}), f32[96,8,128]{2,0,1:T(8,128)S(1)}, u32[]{:S(2)}, u32[]{:S(2)}) async-start(f32[96,8,128]{2,0,1:T(8,128)} %copy.21), calls=%async_computation.3 | async-start | bytes 786432 | tf_op jit(solution)/shard_map/all_to_all | solution.py:109
  545.7 5.5 fusion.1
  551.2 0.0 copy-start.1
  551.2 5.6 copy.20
  556.8 8.3 %convert_element_type.84 = bf16[1,3,96,8192]{3,2,1,0:T(8,128)(2,1)} reshape(bf16[3,96,32,256]{3,2,1,0:T(8,128)(2,1)} %copy.20) | data formatting | bytes 9437184 | tf_op jit(solution)/shard_map/convert_element_type | solution.py:119
  565.1 0.0 all-to-all-done.3
  565.1 0.2 copy.22
  565.3 1.0 gather_fusion.3
  566.4 0.4 reduce_sum.42
  566.7 0.7 copy.23
  567.5 0.0 copy-done.1
  (14 shorter events, 0.1 us)
Async XLA Ops:
  7.2 187.5 %copy-start = (bf16[1,3072,256]{2,1,0:T(8,128)(2,1)S(1)}, bf16[1,3072,256]{2,1,0:T(8,128)(2,1)}, u32[]{:S(2)}) copy-start(bf16[1,3072,256]{2,1,0:T(8,128)(2,1)} %param.11) | copy-start | bytes 4718596
  33.2 8.1 %copy-start.2 = (bf16[256,3072]{1,0:T(8,128)(2,1)S(1)}, bf16[256,3072]{1,0:T(8,128)(2,1)}, u32[]{:S(2)}) copy-start(bf16[256,3072]{1,0:T(8,128)(2,1)} %param.8) | copy-start | bytes 4718596
  33.2 79.4 %all-to-all-start = ((bf16[8,128,3072]{2,1,0:T(8,128)(2,1)}), bf16[8,128,3072]{2,1,0:T(8,128)(2,1)}, u32[]{:S(2)}, u32[]{:S(2)}) async-start(bf16[8,128,3072]{2,1,0:T(8,128)(2,1)} %broadcast_select_fusion), calls=%async_computation | async-start | bytes 12582912 | tf_op jit(solution)/shard_map/all_to_all | solution.py:93
  41.3 6.8 %copy-start.6 = (bf16[256,2]{0,1:T(2,128)(2,1)S(1)}, bf16[256,2]{0,1:T(2,128)(2,1)}, u32[]{:S(2)}) copy-start(bf16[256,2]{0,1:T(2,128)(2,1)} %param.10) | copy-start | bytes 3076
  64.2 54.0 %copy-start.4 = (bf16[1,3072,256]{2,1,0:T(8,128)(2,1)S(1)}, bf16[1,3072,256]{2,1,0:T(8,128)(2,1)}, u32[]{:S(2)}) copy-start(bf16[1,3072,256]{2,1,0:T(8,128)(2,1)} %param.12) | copy-start | bytes 4718596
  112.7 76.9 %all-to-all-start.1 = ((bf16[8,128,3072]{2,1,0:T(8,128)(2,1)}), bf16[8,128,3072]{2,1,0:T(8,128)(2,1)}, u32[]{:S(2)}, u32[]{:S(2)}) async-start(bf16[8,128,3072]{2,1,0:T(8,128)(2,1)} %fusion.3), calls=%async_computation.1 | async-start | bytes 12582912 | tf_op jit(solution)/shard_map/all_to_all | solution.py:94
  118.2 416.3 %reduce-scatter.4.cloned.1.call-start = ((), (), s32[]{:S(2)}) async-start(), calls=%async_computation.5 | async-start | bytes 12976128
  189.6 5.1 copy-start.7
  200.5 1.8 copy-start.5
  225.9 4.8 copy-start.8
  225.9 4.8 copy-start.9
  447.6 2.6 copy-start.3
  536.6 28.5 %all-to-all-start.3 = ((f32[96,8,128]{2,0,1:T(8,128)}), f32[96,8,128]{2,0,1:T(8,128)S(1)}, u32[]{:S(2)}, u32[]{:S(2)}) async-start(f32[96,8,128]{2,0,1:T(8,128)} %copy.21), calls=%async_computation.3 | async-start | bytes 786432 | tf_op jit(solution)/shard_map/all_to_all | solution.py:109
  551.2 16.3 %copy-start.1 = (bf16[1,3072,256]{2,1,0:T(8,128)(2,1)S(1)}, bf16[1,3072,256]{2,1,0:T(8,128)(2,1)}, u32[]{:S(2)}) copy-start(bf16[1,3072,256]{2,1,0:T(8,128)(2,1)} %param.11) | copy-start | bytes 4718596
Sparse Core Ops, SparseCore 0:
  221.3 313.0 reduce-scatter.3
where the time goes:
time: 575 us; the launch traced here: 574 us
  blocking collectives  262 us (46%)
  waiting for transfers between devices  116 us (20%)
  local copies, waits for them, and re-layouts  88.9 us (15%)
  matrix products  39.2 us (7%)
  other arithmetic  30.7 us (5%)
  starting transfers between devices  22.6 us (4%)
  between operations  15 us (3%)
    all_to_all x1, blocking collectives, per_device(): lax.all_to_all(gradients, 'dp', split_axis=1, concat_axis=2, tiled=True)  187 us
    psum x1, blocking collectives, per_device(): lax.psum(jnp.sum(jnp.square(owned_rows.astype(jnp.float32))), ('dp', 'exp...  74.5 us
    all_to_all x1, waiting for transfers between devices, per_device(): lax.all_to_all(weighted_send, 'expert', split_axis=0, concat_axis=0, tile...  65.8 us
    all_to_all x1, waiting for transfers between devices, per_device(): lax.all_to_all(input_send, 'expert', split_axis=0, concat_axis=0, tiled=T...  48.5 us
    another operation x1, local copies, waits for them, and re-layouts, expert_pass(): jnp.stack([row_contract(input_rows, grad_gate), row_contract(input_rows,...  23.9 us
    unnamed x25, local copies, waits for them, and re-layouts  18.1 us
    dot_general x3, matrix products, row_contract(): lax.dot_general(left, right, (((0,), (0,)), ((), ())), preferred_element_...  14.7 us
    convert_element_type x2, local copies, waits for them, and re-layouts, per_device(): clipped = (owned_rows.astype(jnp.float32) * clip_scale).astype(jnp.bfloat16)  13.9 us
  transfers between devices with their start and end apart: 4, of which 3 were waited for; matrix products, arithmetic and copies ran while one was open for 16% of the time, Pallas kernels for 0%

commit v1 on v0

--- a/solution.py
+++ b/solution.py
@@ -112,7 +112,10 @@
         jnp.bfloat16
     )
     gradients = grad_sum.astype(jnp.bfloat16)
-    owned_rows = lax.all_to_all(gradients, "dp", split_axis=1, concat_axis=2, tiled=True)
+    owned_rows = jnp.concatenate(
+        lax.all_to_all(jnp.stack(jnp.split(gradients, lax.axis_size("dp"), axis=1)), "dp", 0, 0),
+        axis=2,
+    )
     squares = lax.psum(jnp.sum(jnp.square(owned_rows.astype(jnp.float32))), ("dp", "expert"))
     clip_limit = CLIP_RMS * math.sqrt(3.0 * experts * model_width * units * shards)
     clip_scale = clip_limit / jnp.maximum(jnp.sqrt(squares), clip_limit)

time: 575 us -> 565 us (0.983)
  waiting for transfers between devices: 116 us -> 175 us
  blocking collectives: 262 us -> 228 us
  local copies, waits for them, and re-layouts: 88.9 us -> 58.1 us
  other arithmetic: 30.7 us -> 24.4 us
    unnamed x2, waiting for transfers between devices: 1.92 us -> 51.2 us
    all_to_all x1, blocking collectives: 187 us -> 153 us  [per_device(): lax.all_to_all(jnp.stack(jnp.split(gradients, lax.axis_size('dp'), axis=1...]
    another operation x2, local copies, waits for them, and re-layouts: 23.9 us -> 0.02 us  [the longest x1 0.01 us: per_device(): jnp.stack(jnp.split(gradients, lax.axis_size('dp'), axis=1))]
    all_to_all x1, waiting for transfers between devices: 48.5 us -> 65.3 us  [per_device(): lax.all_to_all(input_send, 'expert', split_axis=0, concat_axis=0, tiled=T...]
    all_to_all x1, waiting for transfers between devices: 65.8 us -> 58.6 us  [per_device(): lax.all_to_all(weighted_send, 'expert', split_axis=0, concat_axis=0, tile...]
    gather x1, local copies, waits for them, and re-layouts: 13.8 us -> 6.83 us  [fill_rows(): token_block[token_of_slot]]
    unnamed x25 -> x58, local copies, waits for them, and re-layouts: 18.1 us -> 18.9 us
  transfers between devices with their start and end apart: 4 -> 4, of which waited for: 3 -> 3; matrix products, arithmetic and copies ran while one was open for 16% -> 10% of each run, Pallas kernels for 0% -> 0%
where the time goes in v1:
time: 565 us; the launch traced here: 564 us
  blocking collectives  228 us (40%)
  waiting for transfers between devices  175 us (31%)
  local copies, waits for them, and re-layouts  58.1 us (10%)
  matrix products  39.7 us (7%)
  other arithmetic  24.4 us (4%)
  starting transfers between devices  22.8 us (4%)
  between operations  15.3 us (3%)
    all_to_all x1, blocking collectives, per_device(): lax.all_to_all(jnp.stack(jnp.split(gradients, lax.axis_size('dp'), axis=1...  153 us
    psum x1, blocking collectives, per_device(): lax.psum(jnp.sum(jnp.square(owned_rows.astype(jnp.float32))), ('dp', 'exp...  75.7 us
    all_to_all x1, waiting for transfers between devices, per_device(): lax.all_to_all(input_send, 'expert', split_axis=0, concat_axis=0, tiled=T...  65.3 us
    all_to_all x1, waiting for transfers between devices, per_device(): lax.all_to_all(weighted_send, 'expert', split_axis=0, concat_axis=0, tile...  58.6 us
    unnamed x2, waiting for transfers between devices  51.2 us
    unnamed x58, local copies, waits for them, and re-layouts  18.9 us
    dot_general x3, matrix products, row_contract(): lax.dot_general(left, right, (((0,), (0,)), ((), ())), preferred_element_...  14.6 us
    convert_element_type x2, local copies, waits for them, and re-layouts, per_device(): clipped = (owned_rows.astype(jnp.float32) * clip_scale).astype(jnp.bfloat16)  13.2 us
  transfers between devices with their start and end apart: 4, of which 3 were waited for; matrix products, arithmetic and copies ran while one was open for 10% of the time, Pallas kernels for 0%

profile of v1, /device:TPU:1, one launch (start us, length us, event | category | flops | bytes accessed | tf_op | source)
XLA Modules:
  0.0 563.6 jit_solution(6231794232357759737)
XLA Ops:
  7.2 0.0 copy-start
  7.2 0.0 copy-start.2
  7.2 1.0 copy.14
  8.2 0.1 eq.29
  8.3 0.1 eq.25
  8.4 0.7 broadcast_multiply_fusion
  9.1 1.1 reduce-window.6
  10.3 0.2 slice_reduce_fusion
  10.5 0.1 copy.15
  10.7 0.1 mul.66
  10.8 0.1 convert_reduce_fusion
  11.0 2.4 scatter_custom_fusion
  13.5 0.8 copy.17
  14.3 0.2 reshape.127
  14.4 6.8 %gather_fusion.1 = bf16[1024]{0:T(1024)(128)(2,1)S(1)} fusion(bf16[512]{0:T(512)(128)(2,1)S(1)} %reshape.127, s32[1024]{0:T(1024)S(1)} %get-tuple-element.8), kind=kCustom, calls=%fused_computation.1 | custom fusion | bytes 8192 | tf_op jit(solution)/shard_map/gather | solution.py:34
  21.3 0.1 iota_compare_fusion.2
  21.3 0.0 copy-done.2
  21.3 6.8 %gather_fusion.2 = bf16[1024,3072]{1,0:T(8,128)(2,1)} fusion(bf16[256,3072]{1,0:T(8,128)(2,1)S(1)} %copy-done.2, s32[1024]{0:T(1024)S(1)} %get-tuple-element.9), kind=kCustom, calls=%fused_computation.2 | custom fusion | bytes 12587008 | tf_op jit(solution)/shard_map/gather | solution.py:34
  28.2 8.9 %fusion.1 = bf16[8,128,3072]{2,1,0:T(8,128)(2,1)} fusion(bf16[8,128,3072]{2,1,0:T(8,128)(2,1)} %bitcast.186, f32[8,128]{1,0:T(8,128)S(1)} %bitcast_convert_fusion, pred[8,128]{1,0:T(8,128)(4,1)S(1)} %iota_compare_fusion.2), kind=kLoop, calls=%fused_computation.7 | loop fusion | flops 12582912 | bytes 12588032 | tf_op jit(solution)/shard_map/convert_element_type | solution.py:37
  37.1 8.0 %all-to-all-start.1 = ((bf16[8,128,3072]{2,1,0:T(8,128)(2,1)}), bf16[8,128,3072]{2,1,0:T(8,128)(2,1)}, u32[]{:S(2)}, u32[]{:S(2)}) async-start(bf16[8,128,3072]{2,1,0:T(8,128)(2,1)} %fusion.1), calls=%async_computation.1 | async-start | bytes 12582912 | tf_op jit(solution)/shard_map/all_to_all | solution.py:94
  45.2 0.0 copy-done.3
  45.2 6.8 %gather_fusion = bf16[1024,3072]{1,0:T(8,128)(2,1)} fusion(bf16[256,3072]{1,0:T(8,128)(2,1)S(1)} %copy-done.3, s32[1024]{0:T(1024)S(1)} %get-tuple-element.9), kind=kCustom, calls=%fused_computation | custom fusion | bytes 12587008 | tf_op jit(solution)/shard_map/gather | solution.py:32
  52.0 5.9 %broadcast_select_fusion = bf16[8,128,3072]{2,1,0:T(8,128)(2,1)} fusion(bf16[8,128,3072]{2,1,0:T(8,128)(2,1)} %bitcast.185, pred[8,128]{1,0:T(8,128)(4,1)S(1)} %iota_compare_fusion.2), kind=kLoop, calls=%fused_computation.13 | loop fusion | flops 3145728 | bytes 12583936 | tf_op jit(solution)/shard_map/jit(_where)/select_n | solution.py:31
  57.9 58.6 %all-to-all-done.1 = bf16[8,128,3072]{2,1,0:T(8,128)(2,1)} async-done(((bf16[8,128,3072]{2,1,0:T(8,128)(2,1)}), bf16[8,128,3072]{2,1,0:T(8,128)(2,1)}, u32[]{:S(2)}, u32[]{:S(2)}) %all-to-all-start.1) | async-done | bytes 6291488 | tf_op jit(solution)/shard_map/all_to_all | solution.py:94
  116.6 5.5 all-to-all-start
  122.1 0.0 reduce-scatter.4.cloned.1.call-start
  122.1 6.1 %fusion.15 = f32[1024,256]{1,0:T(8,128)} fusion(bf16[1024,3072]{1,0:T(8,128)(2,1)} %bitcast.8, bf16[1,3072,256]{2,1,0:T(8,128)(2,1)} %param.13), kind=kOutput, calls=%fused_computation.29 | convolution fusion | flops 1610612736 | bytes 8912896 | tf_op jit(solution)/shard_map/dot_general | solution.py:65
  128.2 65.3 %all-to-all-done = bf16[8,128,3072]{2,1,0:T(8,128)(2,1)} async-done(((bf16[8,128,3072]{2,1,0:T(8,128)(2,1)}), bf16[8,128,3072]{2,1,0:T(8,128)(2,1)}, u32[]{:S(2)}, u32[]{:S(2)}) %all-to-all-start) | async-done | bytes 6291488 | tf_op jit(solution)/shard_map/all_to_all | solution.py:93
  193.5 0.0 copy-done.5
  193.5 4.7 fusion.13
  198.1 0.0 copy-done
  198.1 0.0 copy-done.9
  198.1 0.0 copy-start.7
  198.2 6.2 %multiply_convert_fusion.2 = (bf16[1024,256]{1,0:T(8,128)(2,1)S(1)}, bf16[1024,256]{1,0:T(8,128)(2,1)S(1)}, f32[1024,256]{1,0:T(8,128)}) fusion(f32[1024,256]{1,0:T(8,128)S(1)} %copy-done.9, f32[1024,256]{1,0:T(8,128)S(1)} %fusion.13, bf16[1024,3072]{1,0:T(8,128)(2,1)} %bitcast.5, bf16[1,3072,256]{2,1,0:T(8,128)(2,1)S(1)} %copy-done), kind=kOutput, calls=%fused_computation.33 | convolution fusion | flops 1614020608 | bytes 12058624 | tf_op jit(solution)/shard_map/dot_general | solution.py:60
  204.3 0.0 copy-done.7
  204.3 1.8 fusion.8
  206.2 0.0 copy-done.6
  206.2 6.3 %add_bitcast_fusion = f32[3072,1024]{0,1:T(8,128)} fusion(f32[1024,3072]{1,0:T(8,128)S(1)} %fusion.8, bf16[1024,256]{1,0:T(8,128)(2,1)S(1)} %get-tuple-element.7, bf16[1,3072,256]{2,1,0:T(8,128)(2,1)S(1)} %copy-done.6), kind=kOutput, calls=%fused_computation.8 | convolution fusion | flops 1613758464 | bytes 27262976 | tf_op jit(solution)/shard_map/dot_general | solution.py:54
  212.5 12.6 %copy.22 = f32[3072,1024]{1,0:T(8,128)} copy(f32[3072,1024]{0,1:T(8,128)} %add_bitcast_fusion) | data formatting | bytes 25165824
  225.0 0.0 reduce-scatter.4.cloned.1.call-update
  225.1 4.7 fusion.5
  229.7 0.0 copy-start.8
  229.8 0.0 copy-start.10
  229.8 4.8 fusion.6
  234.6 0.0 copy-done.8
  234.6 5.1 fusion.7
  239.8 0.6 pad_maximum_fusion
  241.0 152.6 %all_to_all.27 = bf16[32,3,96,256]{3,2,1,0:T(8,128)(2,1)S(1)} all-to-all(bf16[32,3,96,256]{3,2,1,0:T(8,128)(2,1)S(1)} %fusion.19), channel_id=1, replica_groups=mesh['dp'=32,'expert'=8] {'dp'}, dimensions={0} | all-to-all | bytes 9437184 | tf_op jit(solution)/shard_map/all_to_all | solution.py:116
  393.6 2.2 copy-done.4
  395.8 3.0 fusion.2
  398.8 75.7 %psum.7 = f32[]{:T(128)} all-reduce(f32[]{:T(128)} %fusion.2), channel_id=1, replica_groups=mesh['dp'=32,'expert'=8] {'dp','expert'}, use_global_device_ids=true, to_apply=%region_6.7 | all-reduce | flops 1 | bytes 8 | tf_op jit(solution)/shard_map/psum | solution.py:119
  475.2 51.2 %reduce-scatter.4.cloned.1.call-done = f32[96,1024]{1,0:T(8,128)} async-done(((f32[3072,1024]{1,0:T(8,128)}), f32[96,1024]{1,0:T(8,128)}) %reduce-scatter.4.cloned.1.call-update) | async-done | bytes 393232
  526.4 1.2 copy.23
  527.6 1.0 copy.19
  528.6 9.2 %all-to-all-start.3 = ((f32[96,8,128]{2,0,1:T(8,128)}), f32[96,8,128]{2,0,1:T(8,128)S(1)}, u32[]{:S(2)}, u32[]{:S(2)}) async-start(f32[96,8,128]{2,0,1:T(8,128)} %copy.19), calls=%async_computation.3 | async-start | bytes 786432 | tf_op jit(solution)/shard_map/all_to_all | solution.py:109
  537.8 3.5 fusion.4
  541.3 0.0 copy-start.1
  541.3 4.9 copy.18
  546.2 8.3 %convert_element_type.85 = bf16[1,3,96,8192]{3,2,1,0:T(8,128)(2,1)} reshape(bf16[3,96,32,256]{3,2,1,0:T(8,128)(2,1)} %copy.18) | data formatting | bytes 9437184 | tf_op jit(solution)/shard_map/convert_element_type | solution.py:122
  554.5 0.0 all-to-all-done.3
  554.5 0.2 copy.20
  554.7 1.0 gather_fusion.3
  555.7 0.4 reduce_sum.42
  556.1 0.7 copy.21
  (47 shorter events, 0.5 us)
Async XLA Ops:
  7.2 191.0 %copy-start = (bf16[1,3072,256]{2,1,0:T(8,128)(2,1)S(1)}, bf16[1,3072,256]{2,1,0:T(8,128)(2,1)}, u32[]{:S(2)}) copy-start(bf16[1,3072,256]{2,1,0:T(8,128)(2,1)} %param.11) | copy-start | bytes 4718596
  7.2 14.2 %copy-start.2 = (bf16[256,3072]{1,0:T(8,128)(2,1)S(1)}, bf16[256,3072]{1,0:T(8,128)(2,1)}, u32[]{:S(2)}) copy-start(bf16[256,3072]{1,0:T(8,128)(2,1)} %param.8) | copy-start | bytes 4718596
  37.1 8.1 %copy-start.3 = (bf16[256,3072]{1,0:T(8,128)(2,1)S(1)}, bf16[256,3072]{1,0:T(8,128)(2,1)}, u32[]{:S(2)}) copy-start(bf16[256,3072]{1,0:T(8,128)(2,1)} %param.7) | copy-start | bytes 4718596
  37.1 79.4 %all-to-all-start.1 = ((bf16[8,128,3072]{2,1,0:T(8,128)(2,1)}), bf16[8,128,3072]{2,1,0:T(8,128)(2,1)}, u32[]{:S(2)}, u32[]{:S(2)}) async-start(bf16[8,128,3072]{2,1,0:T(8,128)(2,1)} %fusion.1), calls=%async_computation.1 | async-start | bytes 12582912 | tf_op jit(solution)/shard_map/all_to_all | solution.py:94
  116.6 76.9 %all-to-all-start = ((bf16[8,128,3072]{2,1,0:T(8,128)(2,1)}), bf16[8,128,3072]{2,1,0:T(8,128)(2,1)}, u32[]{:S(2)}, u32[]{:S(2)}) async-start(bf16[8,128,3072]{2,1,0:T(8,128)(2,1)} %broadcast_select_fusion), calls=%async_computation | async-start | bytes 12582912 | tf_op jit(solution)/shard_map/all_to_all | solution.py:93
  122.1 404.4 %reduce-scatter.4.cloned.1.call-start = ((), (), s32[]{:S(2)}) async-start(), calls=%async_computation.5 | async-start | bytes 12976128
  122.1 71.4 %copy-start.5 = (bf16[1,3072,256]{2,1,0:T(8,128)(2,1)S(1)}, bf16[1,3072,256]{2,1,0:T(8,128)(2,1)}, u32[]{:S(2)}) copy-start(bf16[1,3072,256]{2,1,0:T(8,128)(2,1)} %param.12) | copy-start | bytes 4718596
  193.5 4.7 copy-start.9
  198.1 6.2 %copy-start.7 = (f32[1024,256]{1,0:T(8,128)}, f32[1024,256]{1,0:T(8,128)S(1)}, u32[]{:S(2)}) copy-start(f32[1024,256]{1,0:T(8,128)S(1)} %fusion.13) | copy-start | bytes 3145732
  204.3 1.8 copy-start.6
  229.7 4.8 copy-start.8
  229.8 4.8 copy-start.10
  393.6 2.2 copy-start.4
  528.6 25.9 %all-to-all-start.3 = ((f32[96,8,128]{2,0,1:T(8,128)}), f32[96,8,128]{2,0,1:T(8,128)S(1)}, u32[]{:S(2)}, u32[]{:S(2)}) async-start(f32[96,8,128]{2,0,1:T(8,128)} %copy.19), calls=%async_computation.3 | async-start | bytes 786432 | tf_op jit(solution)/shard_map/all_to_all | solution.py:109
  541.3 15.5 %copy-start.1 = (bf16[1,3072,256]{2,1,0:T(8,128)(2,1)S(1)}, bf16[1,3072,256]{2,1,0:T(8,128)(2,1)}, u32[]{:S(2)}) copy-start(bf16[1,3072,256]{2,1,0:T(8,128)(2,1)} %param.11) | copy-start | bytes 4718596
Sparse Core Ops, SparseCore 0:
  225.2 301.1 reduce-scatter.3
